TPU v7x, 32 devices: a whole 2x2x4 slice. The times are simulated.
32 devices in a mesh: job: 2 (over y), aux: 16 (over z, x, core).
Axes of the slice: x: 2, y: 2, z: 4, core: 2. Of those that a mesh axis runs over, the one named last changes fastest.
Arguments:
- ints_ov: bfloat16 [256, 384, 384], P(('job', 'aux')), parts along dimension 0, may hold values from -0.3125 to 0.3125
- ints_oo: bfloat16 [256, 2, 384], P(('job', 'aux')), parts along dimension 0, may hold values from -1.5 to 1.5
- trial: bfloat16 [64, 4, 384], P('job'), parts along dimension 0, may hold values from -6 to 6
- occ_energy: float32 [64], P('job'), parts along dimension 0, may hold values from -1 to -0.2
- vir_energy: float32 [32000], P('job'), parts along dimension 0, may hold values from 0.2 to 2.5
- root_shift: float32 [8], P('job'), parts along dimension 0, may hold values from 0.1 to 0.6
- vir_blocks: int32 [32, 3], P('job'), parts along dimension 0, may hold values from 0 to 124, as said below
- pair_list: int32 [32, 4, 2], P('job'), parts along dimension 0, may hold values from 0 to 31, as said below
- pair_count: int32 [32], P('job'), parts along dimension 0, may hold values from 2 to 4, as said below
Outputs:
- sigma: float32 [64, 4, 384], P(('job', 'aux')), parts along dimension 0
There are 2 independent parts, one for each index of `job`. A program takes and returns all parts, laid end to end along the dimension named above; each array names one. Nothing has to cross between parts.
Inputs may be any that keep to these rules, and one draw needn't show every extreme that they name: `pair_count`: some domain has 4 live pairs. `pair_list`: for domain d all 4 slots hold distinct pairs (i, j): i an occupied of domain d (d * 2 to d * 2 + 1) and j an occupied of one of the domains d + 1 to d + 3, taken cyclically modulo 16; slots from pair_count[d] on are not live. `vir_blocks`: the blocks of one domain are distinct.
All inputs are finite; a program needn't handle non-finite values.
Results may differ from a plain program's by a relative error of at most 0.00036.
Values may be sent and summed in bfloat16 or wider, within the bound.
No kernel may reach another device: no remote copies, remote signals or barrier semaphores. Data moves between devices by JAX's collectives and lax.ppermute only.
A program may use at most 128 MiB of HBM per device.

v0:
```python
import functools

import jax
import jax.numpy as jnp
from jax import lax
from jax.experimental import pallas as pl
from jax.experimental.pallas import tpu as pltpu
from jax.sharding import PartitionSpec as P

F32, BF16 = jnp.float32, jnp.bfloat16
LANES = 128


def passed_along(value, axis, steps):
    count = lax.axis_size(axis)
    pairs = [(source, (source + steps) % count) for source in range(count)]
    return lax.ppermute(value, axis, pairs)


def pair_of(pairs, slot, me, ndomain, od):
    first, second = pairs[slot, 0, me], pairs[slot, 1, me]
    partner = lax.div(second, od)
    ahead = lax.rem(partner - me + ndomain, ndomain)
    return first, second, ahead, first - me * od, ahead * od + lax.rem(second, od)


def column(row):
    return jnp.concatenate(
        [
            jnp.broadcast_to(row[:, at : at + LANES], (LANES, LANES)).T
            for at in range(0, row.shape[1], LANES)
        ],
        axis=0,
    )


def spread(w, roots):
    return jnp.concatenate(
        [jnp.broadcast_to(w[l : l + 1], (roots, w.shape[1])) for l in range(w.shape[0])], axis=0
    )


def factors(trial, w, roots):
    od, width = w.shape
    by_trial = [
        jnp.concatenate([trial[l * roots : (l + 1) * roots]] * od, axis=0) for l in range(od)
    ]
    by_w = [jnp.broadcast_to(w[l : l + 1], (od * roots, width)) for l in range(od)]
    return by_trial, by_w


def half_pair(roots, x_trial, x_w, y_trial, y_w, x_levels, y_levels, shifts):
    od, width = x_w.shape
    rows = od * roots
    x_by_trial, x_by_w = factors(x_trial, x_w, roots)
    y_by_trial, y_by_w = factors(y_trial, y_w, roots)
    weight = spread(x_w, roots)
    left = jnp.concatenate([part * weight for part in x_by_trial + x_by_w], axis=0)
    high = left.astype(BF16).astype(F32)
    left = jnp.concatenate([high, left - high], axis=0)
    root_of = lax.rem(lax.broadcasted_iota(jnp.int32, left.shape, 0), roots)
    summed = jnp.zeros((left.shape[0], width), F32)
    x_wide = jnp.concatenate([x_levels] * (width // LANES), axis=1)
    for k in range(roots):
        inverse = pltpu.reciprocal(x_wide + (y_levels - shifts[k]), approx=True).astype(BF16)
        mine = jnp.where(root_of == k, left, 0.0).astype(BF16)
        summed += jnp.dot(mine, inverse, preferred_element_type=F32)
    half = summed.shape[0] // 2
    summed = summed[:half] + summed[half:]
    parts = [
        summed[at * rows : (at + 1) * rows] * other for at, other in enumerate(y_by_w + y_by_trial)
    ]
    return functools.reduce(jnp.add, parts)


def send_kernel(
    ndomain, pairs_hbm, counts_hbm, blocks_hbm, occ_hbm, shift_hbm, ints_hbm, couple_hbm, trial_hbm, vir_hbm,
    *rest,
):
    slab, od, fit = couple_hbm.shape
    roots, width = trial_hbm.shape[1:]
    span = slab // od
    sends, rest = rest[: span - 1], rest[span - 1 :]
    (weights, trials, levels, pairs, counts, blocks, occ, shift, ints, couple, trial, vir, total, x_levels, sems) = rest
    me = lax.axis_index("aux")
    small = [
        pltpu.make_async_copy(source, target, sems.at[at])
        for at, (source, target) in enumerate(
            [
                (blocks_hbm, blocks), (pairs_hbm, pairs), (counts_hbm, counts), (occ_hbm, occ),
                (shift_hbm, shift), (vir_hbm, vir), (couple_hbm, couple),
            ]
        )
    ]
    at = len(small)
    near = [lax.rem(me + ahead, ndomain) for ahead in range(span)]
    some_trial = [
        pltpu.make_async_copy(
            trial_hbm.at[pl.ds(near[ahead] * od, od)], trial.at[ahead], sems.at[at + ahead]
        )
        for ahead in range(span)
    ]
    at += span
    big = [
        pltpu.make_async_copy(ints_hbm.at[row], ints.at[row], sems.at[at + row]) for row in range(slab)
    ]
    for copy in small + some_trial + big:
        copy.start()
    total[...] = jnp.zeros_like(total)
    for copy in small:
        copy.wait()
    for ahead in range(span):
        row = jnp.concatenate(
            [vir[pl.ds(blocks[part, near[ahead]], 1), :] for part in range(blocks.shape[0])], axis=1
        )
        levels[ahead] = row
        if ahead == 0:
            x_levels[...] = column(row)
    for ahead in range(span):
        some_trial[ahead].wait()
        trials[ahead] = jnp.concatenate([trial[ahead, l].astype(F32) for l in range(od)], axis=0)
    couplings = jnp.concatenate([couple[row].astype(F32) for row in range(slab)], axis=0).astype(BF16)
    for row in range(slab):
        big[row].wait()
        found = jnp.dot(couplings, ints[row], preferred_element_type=F32)
        for other in range(od, slab) if row < od else range(od):
            weights[row, other] = found[other * od : (other + 1) * od]

    @pl.loop(0, counts[me])
    def _(slot):
        first, second, ahead, row_i, row_j = pair_of(pairs, slot, me, ndomain, od)
        total[ahead] += half_pair(
            roots, trials[0], weights[row_i, row_j], trials[ahead], weights[row_j, row_i],
            x_levels[...], levels[ahead], [occ[first] + occ[second] + shift[k] for k in range(roots)],
        )

    for ahead, send in enumerate(sends):
        for l in range(od):
            send[l] = total[ahead + 1, l * roots : (l + 1) * roots]


def keep_kernel(
    ndomain, pairs_hbm, counts_hbm, occ_hbm, shift_hbm, weights, trials, levels, kept,
    pairs, counts, occ, shift, total, x_levels, sems,
):
    span, rows, width = trials.shape
    od = weights.shape[2]
    roots = rows // od
    me = lax.axis_index("aux")
    small = [
        pltpu.make_async_copy(source, target, sems.at[at])
        for at, (source, target) in enumerate(
            [(pairs_hbm, pairs), (counts_hbm, counts), (occ_hbm, occ), (shift_hbm, shift)]
        )
    ]
    for copy in small:
        copy.start()
    total[...] = jnp.zeros_like(total)
    for ahead in range(span):
        x_levels[ahead] = column(levels[ahead])
    for copy in small:
        copy.wait()

    @pl.loop(0, counts[me])
    def _(slot):
        first, second, ahead, row_i, row_j = pair_of(pairs, slot, me, ndomain, od)
        total[...] += half_pair(
            roots, trials[ahead], weights[row_j, row_i], trials[0], weights[row_i, row_j],
            x_levels[ahead], levels[0], [occ[first] + occ[second] + shift[k] for k in range(roots)],
        )

    for l in range(od):
        kept[l] = total[l * roots : (l + 1) * roots]


def per_device(
    ints_ov, ints_oo, trial, occ_energy, vir_energy, root_shift, vir_blocks, pair_list, pair_count
):
    slab, od, fit = ints_oo.shape
    roots, width = trial.shape[1:]
    ndomain = lax.axis_size("aux")
    span = slab // od
    level_table = vir_energy.reshape(-1, LANES)
    pairs = jnp.transpose(pair_list, (1, 2, 0))
    blocks = vir_blocks.T
    hbm = pl.BlockSpec(memory_space=pltpu.HBM)
    vmem = pl.BlockSpec(memory_space=pltpu.VMEM)
    part = jax.ShapeDtypeStruct((od, roots, width), F32)
    params = pltpu.CompilerParams(vmem_limit_bytes=40 * 1024 * 1024)
    scalars = [pltpu.SMEM(x.shape, x.dtype) for x in (pairs, pair_count, blocks, occ_energy, root_shift)]
    def stay(*arrays):
        return [pltpu.with_memory_space_constraint(array, pltpu.HBM) for array in arrays]

    *sends, weights, trials, levels = pl.pallas_call(
        functools.partial(send_kernel, ndomain),
        out_shape=[part] * (span - 1)
        + [
            jax.ShapeDtypeStruct((slab, slab, od, width), F32),
            jax.ShapeDtypeStruct((span, od * roots, width), F32),
            jax.ShapeDtypeStruct((span, 1, width), F32),
        ],
        in_specs=[hbm] * 9,
        out_specs=[vmem] * (span + 2),
        scratch_shapes=scalars
        + [
            pltpu.VMEM(ints_ov.shape, BF16),
            pltpu.VMEM(ints_oo.shape, BF16),
            pltpu.VMEM((span, od, roots, width), BF16),
            pltpu.VMEM(level_table.shape, F32),
            pltpu.VMEM((span, od * roots, width), F32),
            pltpu.VMEM((width, LANES), F32),
            pltpu.SemaphoreType.DMA((7 + span + slab,)),
        ],
        compiler_params=params,
        name="to_send",
    )(*stay(pairs, pair_count, blocks, occ_energy, root_shift, ints_ov, ints_oo, trial, level_table))
    arrived = [passed_along(send, "aux", at + 1) for at, send in enumerate(sends)]
    kept = pl.pallas_call(
        functools.partial(keep_kernel, ndomain),
        out_shape=part,
        in_specs=[hbm] * 4 + [vmem] * 3,
        out_specs=vmem,
        scratch_shapes=scalars[:2]
        + scalars[3:]
        + [
            pltpu.VMEM((od * roots, width), F32),
            pltpu.VMEM((span, width, LANES), F32),
            pltpu.SemaphoreType.DMA((4,)),
        ],
        compiler_params=params,
        cost_estimate=pl.CostEstimate(flops=10**9, bytes_accessed=10**6, transcendentals=10**6),
        name="to_keep",
    )(*stay(pairs, pair_count, occ_energy, root_shift), weights, trials, levels)
    return functools.reduce(jnp.add, arrived, kept)


def solution(mesh):
    in_specs = (
        P(("job", "aux"), None, None),
        P(("job", "aux"), None, None),
        P("job", None, None),
        P("job"),
        P("job"),
        P("job"),
        P("job", None),
        P("job", None, None),
        P("job"),
    )
    out_specs = P(("job", "aux"), None, None)
    return jax.shard_map(
        per_device, mesh=mesh, in_specs=in_specs, out_specs=out_specs, check_vma=False
    )
```

profile of v0, /device:TPU:1, one launch (start us, length us, event | category | flops | bytes accessed | tf_op | source)
XLA Modules:
  0.0 14.5 jit_solution(1699722648048183469)
XLA Ops:
  0.0 3.6 %to_send.1 = (f32[2,4,384]{2,1,0:T(4,128)S(1)}, f32[2,4,384]{2,1,0:T(4,128)S(1)}, f32[2,4,384]{2,1,0:T(4,128)S(1)}, f32[8,8,2,384]{3,2,1,0:T(2,128)S(1)}, f32[4,...) custom-call(s32[4,2,16]{2,1,0:T(2,128)} %bitcast.13, s32[16]{0:T(128)} %counts_hbm.3, s32[3,16]{1,0:T(4,128)} %bitcast.15, ...), custom_call_target="tpu_custom_call" | custom-call | tf_op jit(solution)/shard_map/to_send/pallas_call | solution.py:194
  3.7 2.7 %collective-permute-start = (f32[2,4,384]{2,1,0:T(4,128)S(1)}, f32[2,4,384]{2,1,0:T(4,128)S(1)}, u32[]{:S(2)}, u32[]{:S(2)}) collective-permute-start(f32[2,4,384]{2,1,0:T(4,128)S(1)} %get-tuple-element.14), channel_id=1, source_target_pairs={{0,1},{1,2},{2,3},{3,4},{4,5},{5,6},{6,7},{7,8},{8,9},{9,10},{10,1... | collective-permute-start | bytes 36872 | tf_op jit(solution)/shard_map/ppermute | solution.py:17
  6.3 1.8 %collective-permute-start.1 = (f32[2,4,384]{2,1,0:T(4,128)S(1)}, f32[2,4,384]{2,1,0:T(4,128)S(1)}, u32[]{:S(2)}, u32[]{:S(2)}) collective-permute-start(f32[2,4,384]{2,1,0:T(4,128)S(1)} %get-tuple-element.15), channel_id=1, source_target_pairs={{0,2},{1,3},{2,4},{3,5},{4,6},{5,7},{6,8},{7,9},{8,10},{9,11},{10,... | collective-permute-start | bytes 36872 | tf_op jit(solution)/shard_map/ppermute | solution.py:17
  8.1 0.7 %collective-permute-start.2 = (f32[2,4,384]{2,1,0:T(4,128)S(1)}, f32[2,4,384]{2,1,0:T(4,128)S(1)}, u32[]{:S(2)}, u32[]{:S(2)}) collective-permute-start(f32[2,4,384]{2,1,0:T(4,128)S(1)} %get-tuple-element.16), channel_id=1, source_target_pairs={{0,3},{1,4},{2,5},{3,6},{4,7},{5,8},{6,9},{7,10},{8,11},{9,12},{10... | collective-permute-start | bytes 36872 | tf_op jit(solution)/shard_map/ppermute | solution.py:17
  8.8 1.8 %to_keep.1 = f32[2,4,384]{2,1,0:T(4,128)S(1)} custom-call(s32[4,2,16]{2,1,0:T(2,128)} %bitcast.14, s32[16]{0:T(128)} %counts_hbm.3, f32[32]{0:T(128)} %occ_hbm.3, f32[4]{0:T(128)} %shift_hbm.3, f32[8,8,2,384]{3,2,1,0:T(2,128)S(1)} %get-tuple-element.11.weights, f32[4,8,384]{2,1,0:T(8,128)S(1)} %get-tuple-element.12.trials, ...), custom_call_target="tpu_custom_call" | custom-call | flops 1000000000 | bytes 1000000 | tf_op jit(solution)/shard_map/to_keep/pallas_call | solution.py:218
  10.6 0.0 collective-permute-done
  10.6 1.0 %collective-permute-done.1 = f32[2,4,384]{2,1,0:T(4,128)S(1)} collective-permute-done((f32[2,4,384]{2,1,0:T(4,128)S(1)}, f32[2,4,384]{2,1,0:T(4,128)S(1)}, u32[]{:S(2)}, u32[]{:S(2)}) %collective-permute-start.1) | collective-permute-done | bytes 12320 | tf_op jit(solution)/shard_map/ppermute | solution.py:17
  11.6 2.3 %collective-permute-done.2 = f32[2,4,384]{2,1,0:T(4,128)S(1)} collective-permute-done((f32[2,4,384]{2,1,0:T(4,128)S(1)}, f32[2,4,384]{2,1,0:T(4,128)S(1)}, u32[]{:S(2)}, u32[]{:S(2)}) %collective-permute-start.2) | collective-permute-done | bytes 12320 | tf_op jit(solution)/shard_map/ppermute | solution.py:17
  13.9 0.6 %add_add_fusion = f32[1,8,384]{2,1,0:T(8,128)} fusion(f32[1,8,384]{2,1,0:T(8,128)S(1)} %bitcast.12, f32[1,8,384]{2,1,0:T(8,128)S(1)} %bitcast.11, f32[1,8,384]{2,1,0:T(8,128)S(1)} %bitcast.8, f32[1,8,384]{2,1,0:T(8,128)S(1)} %bitcast.10), kind=kLoop, calls=%fused_computation | loop fusion | flops 9216 | bytes 61440 | tf_op jit(solution)/shard_map/add | solution.py:234
Async XLA Ops:
  3.7 6.9 %collective-permute-start = (f32[2,4,384]{2,1,0:T(4,128)S(1)}, f32[2,4,384]{2,1,0:T(4,128)S(1)}, u32[]{:S(2)}, u32[]{:S(2)}) collective-permute-start(f32[2,4,384]{2,1,0:T(4,128)S(1)} %get-tuple-element.14), channel_id=1, source_target_pairs={{0,1},{1,2},{2,3},{3,4},{4,5},{5,6},{6,7},{7,8},{8,9},{9,10},{10,1... | collective-permute-start | bytes 36872 | tf_op jit(solution)/shard_map/ppermute | solution.py:17
  6.3 5.3 %collective-permute-start.1 = (f32[2,4,384]{2,1,0:T(4,128)S(1)}, f32[2,4,384]{2,1,0:T(4,128)S(1)}, u32[]{:S(2)}, u32[]{:S(2)}) collective-permute-start(f32[2,4,384]{2,1,0:T(4,128)S(1)} %get-tuple-element.15), channel_id=1, source_target_pairs={{0,2},{1,3},{2,4},{3,5},{4,6},{5,7},{6,8},{7,9},{8,10},{9,11},{10,... | collective-permute-start | bytes 36872 | tf_op jit(solution)/shard_map/ppermute | solution.py:17
  8.1 5.8 %collective-permute-start.2 = (f32[2,4,384]{2,1,0:T(4,128)S(1)}, f32[2,4,384]{2,1,0:T(4,128)S(1)}, u32[]{:S(2)}, u32[]{:S(2)}) collective-permute-start(f32[2,4,384]{2,1,0:T(4,128)S(1)} %get-tuple-element.16), channel_id=1, source_target_pairs={{0,3},{1,4},{2,5},{3,6},{4,7},{5,8},{6,9},{7,10},{8,11},{9,12},{10... | collective-permute-start | bytes 36872 | tf_op jit(solution)/shard_map/ppermute | solution.py:17
where the time goes:
time: 14.5 us
  Pallas kernels  5.48 us (38%)
  starting transfers between devices  5.09 us (35%)
  waiting for transfers between devices  3.31 us (23%)
  other arithmetic  0.6 us (4%)
    ppermute x3, starting transfers between devices, passed_along(): return lax.ppermute(value, axis, pairs)  5.09 us
    pallas_call x1, Pallas kernels, per_device(): pl.pallas_call(functools.partial(send_kernel, ndomain), out_shape=[part]...  3.65 us
    ppermute x3, waiting for transfers between devices, passed_along(): return lax.ppermute(value, axis, pairs)  3.31 us
    pallas_call x1, Pallas kernels, per_device(): pl.pallas_call(functools.partial(keep_kernel, ndomain), out_shape=part, i...  1.83 us
    add x1, other arithmetic, per_device(): return functools.reduce(jnp.add, arrived, kept)  0.6 us
  transfers between devices with their start and end apart: 3, of which 2 were waited for; matrix products, arithmetic and copies ran while one was open for 0% of the time, Pallas kernels for 13%

commit v1 on v0

v1 whole, which is shorter than its diff:
```python
import functools

import jax
import jax.numpy as jnp
from jax import lax
from jax.experimental import pallas as pl
from jax.experimental.pallas import tpu as pltpu
from jax.sharding import PartitionSpec as P

F32, BF16 = jnp.float32, jnp.bfloat16
LANES = 128


def passed_along(value, axis, steps):
    count = lax.axis_size(axis)
    pairs = [(source, (source + steps) % count) for source in range(count)]
    return lax.ppermute(value, axis, pairs)


def column(row):
    return jnp.concatenate(
        [
            jnp.broadcast_to(row[:, at : at + LANES], (LANES, LANES)).T
            for at in range(0, row.shape[1], LANES)
        ],
        axis=0,
    )


def spread(w, roots):
    return jnp.concatenate(
        [jnp.broadcast_to(w[l : l + 1], (roots, w.shape[1])) for l in range(w.shape[0])], axis=0
    )


def factors(trial, w, roots):
    od, width = w.shape
    by_trial = [
        jnp.concatenate([trial[l * roots : (l + 1) * roots]] * od, axis=0) for l in range(od)
    ]
    by_w = [jnp.broadcast_to(w[l : l + 1], (od * roots, width)) for l in range(od)]
    return by_trial, by_w


def root_shifts(pairs, occ, shift, slot, me, roots):
    energy = occ[pairs[slot, 0, me]] + occ[pairs[slot, 1, me]]
    return [energy + shift[k] for k in range(roots)]


def invert(target, x_levels, y_levels, shifts, step=64):
    width = y_levels.shape[1]
    roots = len(shifts)
    for k in range(0, roots, 2):
        for at in range(0, width, step):
            x_wide = jnp.concatenate([x_levels[at : at + step]] * (width // LANES), axis=1)
            one = x_wide + (y_levels - shifts[k])
            if k + 1 == roots:
                found = [pltpu.reciprocal(one, approx=True)]
            else:
                two = x_wide + (y_levels - shifts[k + 1])
                both = pltpu.reciprocal(one * two, approx=True)
                found = [both * two, both * one]
            for more, value in enumerate(found):
                start = (k + more) * width + at
                target[start : start + step] = value.astype(BF16)


def contract(roots, x_trial, x_w, y_trial, y_w, inverse):
    od, width = x_w.shape
    rows = od * roots
    x_by_trial, x_by_w = factors(x_trial, x_w, roots)
    y_by_trial, y_by_w = factors(y_trial, y_w, roots)
    weight = spread(x_w, roots)
    left = jnp.concatenate([part * weight for part in x_by_trial + x_by_w], axis=0)
    high = left.astype(BF16).astype(F32)
    left = jnp.concatenate([high, left - high], axis=0)
    root_of = lax.rem(lax.broadcasted_iota(jnp.int32, left.shape, 0), roots)
    left = jnp.concatenate(
        [jnp.where(root_of == k, left, 0.0).astype(BF16) for k in range(roots)], axis=1
    )
    summed = jnp.dot(left, inverse, preferred_element_type=F32)
    half = summed.shape[0] // 2
    summed = summed[:half] + summed[half:]
    parts = [
        summed[at * rows : (at + 1) * rows] * other for at, other in enumerate(y_by_w + y_by_trial)
    ]
    return functools.reduce(jnp.add, parts)


def send_kernel(
    ndomain, sure, pairs_hbm, counts_hbm, blocks_hbm, occ_hbm, shift_hbm, ints_hbm, couple_hbm, trial_hbm, vir_hbm,
    *rest,
):
    slab, od, fit = couple_hbm.shape
    roots, width = trial_hbm.shape[1:]
    span = slab // od
    slots = pairs_hbm.shape[0]
    sends, rest = rest[: span - 1], rest[span - 1 :]
    (first_w, second_w, trials, levels, pairs, counts, blocks, occ, shift, own_ints, pair_ints, couple, trial, vir,
     own_w, pair_w, total, x_levels, inverse, sems) = rest
    me = lax.axis_index("aux")
    near = [lax.rem(me + ahead, ndomain) for ahead in range(span)]
    wanted = [(pairs_hbm, pairs), (counts_hbm, counts), (blocks_hbm, blocks), (vir_hbm, vir), (occ_hbm, occ),
              (shift_hbm, shift), (couple_hbm, couple)]
    wanted += [(trial_hbm.at[pl.ds(near[ahead] * od, od)], trial.at[ahead]) for ahead in range(span)]
    wanted += [(ints_hbm.at[row], own_ints.at[row]) for row in range(od)]
    copies = [pltpu.make_async_copy(source, target, sems.at[at]) for at, (source, target) in enumerate(wanted)]
    got_pairs, got_counts, got_blocks, got_vir, got_occ, got_shift, got_couple = copies[:7]
    got_trial, got_own = copies[7 : 7 + span], copies[7 + span :]
    for copy in copies:
        copy.start()
    total[...] = jnp.zeros_like(total)

    def where(slot):
        second = pairs[slot, 1, me]
        ahead = lax.rem(lax.div(second, od) - me + ndomain, ndomain)
        return ahead, pairs[slot, 0, me] - me * od, ahead * od + lax.rem(second, od)

    def second_ints(slot):
        return pltpu.make_async_copy(
            ints_hbm.at[where(slot)[2]], pair_ints.at[slot], sems.at[len(copies) + slot]
        )

    got_pairs.wait()
    for slot in range(sure):
        second_ints(slot).start()
    got_counts.wait()
    count = counts[me]
    for slot in range(sure, slots):
        pl.when(count > slot)(lambda slot=slot: second_ints(slot).start())
    got_blocks.wait()
    got_vir.wait()
    for ahead in range(span):
        levels[ahead] = jnp.concatenate(
            [vir[pl.ds(blocks[part, near[ahead]], 1), :] for part in range(blocks.shape[0])], axis=1
        )
    x_levels[...] = column(levels[0])
    got_occ.wait()
    got_shift.wait()

    def prepare(slot):
        invert(
            inverse.at[slot], x_levels, levels[where(slot)[0]],
            root_shifts(pairs, occ, shift, slot, me, roots),
        )

    for slot in range(sure):
        prepare(slot)
    for slot in range(sure, slots):
        pl.when(count > slot)(lambda slot=slot: prepare(slot))
    for ahead in range(span):
        got_trial[ahead].wait()
        trials[ahead] = jnp.concatenate([trial[ahead, l].astype(F32) for l in range(od)], axis=0)
    got_couple.wait()
    couplings = jnp.concatenate([couple[row].astype(F32) for row in range(slab)], axis=0).astype(BF16)
    for row in range(od):
        got_own[row].wait()
        found = jnp.dot(couplings, own_ints[row], preferred_element_type=F32)
        for other in range(od, slab):
            own_w[row, other] = found[other * od : (other + 1) * od]

    def weigh(slot):
        second_ints(slot).wait()
        found = jnp.dot(couplings, pair_ints[slot], preferred_element_type=F32)
        for other in range(od):
            pair_w[slot, other] = found[other * od : (other + 1) * od]

    def add(slot):
        ahead, row_i, row_j = where(slot)
        first_w[slot] = own_w[row_i, row_j]
        second_w[slot] = pair_w[slot, row_i]
        found = contract(
            roots, trials[0], first_w[slot], trials[ahead], second_w[slot], inverse[slot]
        )
        total[ahead] += jnp.where(count > slot, found, 0.0)

    for slot in range(sure):
        weigh(slot)
    for slot in range(sure):
        add(slot)
    for slot in range(sure, slots):

        @pl.when(count > slot)
        def _(slot=slot):
            weigh(slot)
            add(slot)

    for ahead, send in enumerate(sends):
        for l in range(od):
            send[l] = total[ahead + 1, l * roots : (l + 1) * roots]


def keep_kernel(
    ndomain, pairs_hbm, counts_hbm, occ_hbm, shift_hbm, first_w, second_w, trials, levels, kept,
    pairs, counts, occ, shift, total, x_levels, inverse, sems,
):
    span, rows, width = trials.shape
    od = first_w.shape[1]
    roots = rows // od
    me = lax.axis_index("aux")
    small = [
        pltpu.make_async_copy(source, target, sems.at[at])
        for at, (source, target) in enumerate(
            [(pairs_hbm, pairs), (counts_hbm, counts), (occ_hbm, occ), (shift_hbm, shift)]
        )
    ]
    for copy in small:
        copy.start()
    total[...] = jnp.zeros_like(total)
    for ahead in range(span):
        x_levels[ahead] = column(levels[ahead])
    for copy in small:
        copy.wait()

    @pl.loop(0, counts[me])
    def _(slot):
        ahead = lax.rem(lax.div(pairs[slot, 1, me], od) - me + ndomain, ndomain)
        invert(inverse, x_levels.at[ahead], levels[0], root_shifts(pairs, occ, shift, slot, me, roots))
        total[...] += contract(
            roots, trials[ahead], second_w[slot], trials[0], first_w[slot], inverse[...]
        )

    for l in range(od):
        kept[l] = total[l * roots : (l + 1) * roots]


def per_device(
    ints_ov, ints_oo, trial, occ_energy, vir_energy, root_shift, vir_blocks, pair_list, pair_count
):
    slab, od, fit = ints_oo.shape
    roots, width = trial.shape[1:]
    ndomain = lax.axis_size("aux")
    span = slab // od
    level_table = vir_energy.reshape(-1, LANES)
    pairs = jnp.transpose(pair_list, (1, 2, 0))
    blocks = vir_blocks.T
    hbm = pl.BlockSpec(memory_space=pltpu.HBM)
    vmem = pl.BlockSpec(memory_space=pltpu.VMEM)
    part = jax.ShapeDtypeStruct((od, roots, width), F32)
    params = pltpu.CompilerParams(vmem_limit_bytes=40 * 1024 * 1024)
    scalars = [pltpu.SMEM(x.shape, x.dtype) for x in (pairs, pair_count, blocks, occ_energy, root_shift)]
    def stay(*arrays):
        return [pltpu.with_memory_space_constraint(array, pltpu.HBM) for array in arrays]

    slots = pair_list.shape[1]
    sure = min(2, slots)
    *sends, first_w, second_w, trials, levels = pl.pallas_call(
        functools.partial(send_kernel, ndomain, sure),
        out_shape=[part] * (span - 1)
        + [
            jax.ShapeDtypeStruct((slots, od, width), F32),
            jax.ShapeDtypeStruct((slots, od, width), F32),
            jax.ShapeDtypeStruct((span, od * roots, width), F32),
            jax.ShapeDtypeStruct((span, 1, width), F32),
        ],
        in_specs=[hbm] * 9,
        out_specs=[vmem] * (span + 3),
        scratch_shapes=scalars
        + [
            pltpu.VMEM((od, fit, width), BF16),
            pltpu.VMEM((slots, fit, width), BF16),
            pltpu.VMEM(ints_oo.shape, BF16),
            pltpu.VMEM((span, od, roots, width), BF16),
            pltpu.VMEM(level_table.shape, F32),
            pltpu.VMEM((od, slab, od, width), F32),
            pltpu.VMEM((slots, od, od, width), F32),
            pltpu.VMEM((span, od * roots, width), F32),
            pltpu.VMEM((width, LANES), F32),
            pltpu.VMEM((slots, roots * width, width), BF16),
            pltpu.SemaphoreType.DMA((7 + span + od + slots,)),
        ],
        compiler_params=params,
        name="to_send",
    )(*stay(pairs, pair_count, blocks, occ_energy, root_shift, ints_ov, ints_oo, trial, level_table))
    arrived = [passed_along(send, "aux", at + 1) for at, send in enumerate(sends)]
    kept = pl.pallas_call(
        functools.partial(keep_kernel, ndomain),
        out_shape=part,
        in_specs=[hbm] * 4 + [vmem] * 4,
        out_specs=vmem,
        scratch_shapes=scalars[:2]
        + scalars[3:]
        + [
            pltpu.VMEM((od * roots, width), F32),
            pltpu.VMEM((span, width, LANES), F32),
            pltpu.VMEM((roots * width, width), BF16),
            pltpu.SemaphoreType.DMA((4,)),
        ],
        compiler_params=params,
        cost_estimate=pl.CostEstimate(flops=10**9, bytes_accessed=10**6, transcendentals=10**6),
        name="to_keep",
    )(*stay(pairs, pair_count, occ_energy, root_shift), first_w, second_w, trials, levels)
    return functools.reduce(jnp.add, arrived, kept)


def solution(mesh):
    in_specs = (
        P(("job", "aux"), None, None),
        P(("job", "aux"), None, None),
        P("job", None, None),
        P("job"),
        P("job"),
        P("job"),
        P("job", None),
        P("job", None, None),
        P("job"),
    )
    out_specs = P(("job", "aux"), None, None)
    return jax.shard_map(
        per_device, mesh=mesh, in_specs=in_specs, out_specs=out_specs, check_vma=False
    )
```

time: 14.5 us -> 13.8 us (0.952)
  Pallas kernels: 5.48 us -> 4.82 us
  starting transfers between devices: 5.09 us -> 4.58 us
  waiting for transfers between devices: 3.31 us -> 3.82 us
    pallas_call x1, Pallas kernels: 3.65 us -> 2.84 us  [per_device(): pl.pallas_call(functools.partial(send_kernel, ndomain, sure), out_shape=[...]
    ppermute x3, starting transfers between devices: 5.09 us -> 4.58 us  [passed_along(): return lax.ppermute(value, axis, pairs)]
    ppermute x3, waiting for transfers between devices: 3.31 us -> 3.82 us  [passed_along(): return lax.ppermute(value, axis, pairs)]
  transfers between devices with their start and end apart: 3 -> 3, of which waited for: 2 -> 2; matrix products, arithmetic and copies ran while one was open for 0% -> 0% of each run, Pallas kernels for 13% -> 14%
where the time goes in v1:
time: 13.8 us; the launch traced here: 13.9 us
  Pallas kernels  4.82 us (35%)
  starting transfers between devices  4.58 us (33%)
  waiting for transfers between devices  3.82 us (28%)
  other arithmetic  0.6 us (4%)
    ppermute x3, starting transfers between devices, passed_along(): return lax.ppermute(value, axis, pairs)  4.58 us
    ppermute x3, waiting for transfers between devices, passed_along(): return lax.ppermute(value, axis, pairs)  3.82 us
    pallas_call x1, Pallas kernels, per_device(): pl.pallas_call(functools.partial(send_kernel, ndomain, sure), out_shape=[...  2.84 us
    pallas_call x1, Pallas kernels, per_device(): pl.pallas_call(functools.partial(keep_kernel, ndomain), out_shape=part, i...  1.98 us
    add x1, other arithmetic, per_device(): return functools.reduce(jnp.add, arrived, kept)  0.6 us
  transfers between devices with their start and end apart: 3, of which 2 were waited for; matrix products, arithmetic and copies ran while one was open for 0% of the time, Pallas kernels for 14%

profile of v1, /device:TPU:1, one launch (start us, length us, event | category | flops | bytes accessed | tf_op | source)
XLA Modules:
  0.0 13.9 jit_solution(2941171700507789346)
XLA Ops:
  0.0 2.8 %to_send.1 = (f32[2,4,384]{2,1,0:T(4,128)S(1)}, f32[2,4,384]{2,1,0:T(4,128)S(1)}, f32[2,4,384]{2,1,0:T(4,128)S(1)}, f32[4,2,384]{2,1,0:T(2,128)S(1)}, f32[4,2,38...) custom-call(s32[4,2,16]{2,1,0:T(2,128)} %bitcast.13, s32[16]{0:T(128)} %counts_hbm.3, ...), custom_call_target="tpu_custom_call" | custom-call | tf_op jit(solution)/shard_map/to_send/pallas_call | solution.py:247
  2.9 2.7 %collective-permute-start = (f32[2,4,384]{2,1,0:T(4,128)S(1)}, f32[2,4,384]{2,1,0:T(4,128)S(1)}, u32[]{:S(2)}, u32[]{:S(2)}) collective-permute-start(f32[2,4,384]{2,1,0:T(4,128)S(1)} %get-tuple-element.16), channel_id=1, source_target_pairs={{0,1},{1,2},{2,3},{3,4},{4,5},{5,6},{6,7},{7,8},{8,9},{9,10},{10,1... | collective-permute-start | bytes 36872 | tf_op jit(solution)/shard_map/ppermute | solution.py:17
  5.5 1.9 %collective-permute-start.1 = (f32[2,4,384]{2,1,0:T(4,128)S(1)}, f32[2,4,384]{2,1,0:T(4,128)S(1)}, u32[]{:S(2)}, u32[]{:S(2)}) collective-permute-start(f32[2,4,384]{2,1,0:T(4,128)S(1)} %get-tuple-element.17), channel_id=1, source_target_pairs={{0,2},{1,3},{2,4},{3,5},{4,6},{5,7},{6,8},{7,9},{8,10},{9,11},{10,... | collective-permute-start | bytes 36872 | tf_op jit(solution)/shard_map/ppermute | solution.py:17
  7.4 0.0 collective-permute-start.2
  7.4 2.0 %to_keep.1 = f32[2,4,384]{2,1,0:T(4,128)S(1)} custom-call(s32[4,2,16]{2,1,0:T(2,128)} %bitcast.14, s32[16]{0:T(128)} %counts_hbm.3, f32[32]{0:T(128)} %occ_hbm.3, f32[4]{0:T(128)} %shift_hbm.3, f32[4,2,384]{2,1,0:T(2,128)S(1)} %get-tuple-element.12.first_w, f32[4,2,384]{2,1,0:T(2,128)S(1)} %get-tuple-element.13.second_w, ...), custom_call_target="tpu_custom_call" | custom-call | flops 1000000000 | bytes 1000000 | tf_op jit(solution)/shard_map/to_keep/pallas_call | solution.py:276
  9.4 0.0 collective-permute-done
  9.4 1.3 %collective-permute-done.1 = f32[2,4,384]{2,1,0:T(4,128)S(1)} collective-permute-done((f32[2,4,384]{2,1,0:T(4,128)S(1)}, f32[2,4,384]{2,1,0:T(4,128)S(1)}, u32[]{:S(2)}, u32[]{:S(2)}) %collective-permute-start.1) | collective-permute-done | bytes 12320 | tf_op jit(solution)/shard_map/ppermute | solution.py:17
  10.7 2.5 %collective-permute-done.2 = f32[2,4,384]{2,1,0:T(4,128)S(1)} collective-permute-done((f32[2,4,384]{2,1,0:T(4,128)S(1)}, f32[2,4,384]{2,1,0:T(4,128)S(1)}, u32[]{:S(2)}, u32[]{:S(2)}) %collective-permute-start.2) | collective-permute-done | bytes 12320 | tf_op jit(solution)/shard_map/ppermute | solution.py:17
  13.2 0.6 %add_add_fusion = f32[1,8,384]{2,1,0:T(8,128)} fusion(f32[1,8,384]{2,1,0:T(8,128)S(1)} %bitcast.12, f32[1,8,384]{2,1,0:T(8,128)S(1)} %bitcast.11, f32[1,8,384]{2,1,0:T(8,128)S(1)} %bitcast.8, f32[1,8,384]{2,1,0:T(8,128)S(1)} %bitcast.10), kind=kLoop, calls=%fused_computation | loop fusion | flops 9216 | bytes 61440 | tf_op jit(solution)/shard_map/add | solution.py:293
Async XLA Ops:
  2.9 6.6 %collective-permute-start = (f32[2,4,384]{2,1,0:T(4,128)S(1)}, f32[2,4,384]{2,1,0:T(4,128)S(1)}, u32[]{:S(2)}, u32[]{:S(2)}) collective-permute-start(f32[2,4,384]{2,1,0:T(4,128)S(1)} %get-tuple-element.16), channel_id=1, source_target_pairs={{0,1},{1,2},{2,3},{3,4},{4,5},{5,6},{6,7},{7,8},{8,9},{9,10},{10,1... | collective-permute-start | bytes 36872 | tf_op jit(solution)/shard_map/ppermute | solution.py:17
  5.5 5.2 %collective-permute-start.1 = (f32[2,4,384]{2,1,0:T(4,128)S(1)}, f32[2,4,384]{2,1,0:T(4,128)S(1)}, u32[]{:S(2)}, u32[]{:S(2)}) collective-permute-start(f32[2,4,384]{2,1,0:T(4,128)S(1)} %get-tuple-element.17), channel_id=1, source_target_pairs={{0,2},{1,3},{2,4},{3,5},{4,6},{5,7},{6,8},{7,9},{8,10},{9,11},{10,... | collective-permute-start | bytes 36872 | tf_op jit(solution)/shard_map/ppermute | solution.py:17
  7.4 5.8 %collective-permute-start.2 = (f32[2,4,384]{2,1,0:T(4,128)S(1)}, f32[2,4,384]{2,1,0:T(4,128)S(1)}, u32[]{:S(2)}, u32[]{:S(2)}) collective-permute-start(f32[2,4,384]{2,1,0:T(4,128)S(1)} %get-tuple-element.18), channel_id=1, source_target_pairs={{0,3},{1,4},{2,5},{3,6},{4,7},{5,8},{6,9},{7,10},{8,11},{9,12},{10... | collective-permute-start | bytes 36872 | tf_op jit(solution)/shard_map/ppermute | solution.py:17

commit v2 on v1

--- a/solution.py
+++ b/solution.py
@@ -13,8 +13,16 @@
 
 def passed_along(value, axis, steps):
     count = lax.axis_size(axis)
-    pairs = [(source, (source + steps) % count) for source in range(count)]
+    pairs = [(source, (source + steps[source % 2]) % count) for source in range(count)]
     return lax.ppermute(value, axis, pairs)
+
+
+def plan_of(span, count):
+    ahead = range(1, span)
+    if count % 2:
+        return [(steps, steps) for steps in ahead]
+    odd = [steps for steps in ahead if steps % 2]
+    return [(steps, steps) for steps in ahead if steps % 2 == 0] + list(zip(odd[::-1], odd))
 
 
 def column(row):
@@ -88,7 +96,7 @@
 
 
 def send_kernel(
-    ndomain, sure, pairs_hbm, counts_hbm, blocks_hbm, occ_hbm, shift_hbm, ints_hbm, couple_hbm, trial_hbm, vir_hbm,
+    ndomain, sure, plan, pairs_hbm, counts_hbm, blocks_hbm, occ_hbm, shift_hbm, ints_hbm, couple_hbm, trial_hbm, vir_hbm,
     *rest,
 ):
     slab, od, fit = couple_hbm.shape
@@ -144,20 +152,21 @@
             root_shifts(pairs, occ, shift, slot, me, roots),
         )
 
-    for slot in range(sure):
-        prepare(slot)
-    for slot in range(sure, slots):
-        pl.when(count > slot)(lambda slot=slot: prepare(slot))
     for ahead in range(span):
         got_trial[ahead].wait()
         trials[ahead] = jnp.concatenate([trial[ahead, l].astype(F32) for l in range(od)], axis=0)
     got_couple.wait()
     couplings = jnp.concatenate([couple[row].astype(F32) for row in range(slab)], axis=0).astype(BF16)
+    for copy in got_own:
+        copy.wait()
     for row in range(od):
-        got_own[row].wait()
         found = jnp.dot(couplings, own_ints[row], preferred_element_type=F32)
         for other in range(od, slab):
             own_w[row, other] = found[other * od : (other + 1) * od]
+    for slot in range(sure):
+        prepare(slot)
+    for slot in range(sure, slots):
+        pl.when(count > slot)(lambda slot=slot: prepare(slot))
 
     def weigh(slot):
         second_ints(slot).wait()
@@ -185,9 +194,10 @@
             weigh(slot)
             add(slot)
 
-    for ahead, send in enumerate(sends):
+    for (even, odd), send in zip(plan, sends):
+        ahead = jnp.where(lax.rem(me, 2) == 0, even, odd)
         for l in range(od):
-            send[l] = total[ahead + 1, l * roots : (l + 1) * roots]
+            send[l] = total[ahead, l * roots : (l + 1) * roots]
 
 
 def keep_kernel(
@@ -207,7 +217,7 @@
     for copy in small:
         copy.start()
     total[...] = jnp.zeros_like(total)
-    for ahead in range(span):
+    for ahead in range(1, span):
         x_levels[ahead] = column(levels[ahead])
     for copy in small:
         copy.wait()
@@ -244,8 +254,9 @@
 
     slots = pair_list.shape[1]
     sure = min(2, slots)
+    plan = plan_of(span, ndomain)
     *sends, first_w, second_w, trials, levels = pl.pallas_call(
-        functools.partial(send_kernel, ndomain, sure),
+        functools.partial(send_kernel, ndomain, sure, plan),
         out_shape=[part] * (span - 1)
         + [
             jax.ShapeDtypeStruct((slots, od, width), F32),
@@ -272,7 +283,7 @@
         compiler_params=params,
         name="to_send",
     )(*stay(pairs, pair_count, blocks, occ_energy, root_shift, ints_ov, ints_oo, trial, level_table))
-    arrived = [passed_along(send, "aux", at + 1) for at, send in enumerate(sends)]
+    arrived = [passed_along(send, "aux", steps) for send, steps in zip(sends, plan)]
     kept = pl.pallas_call(
         functools.partial(keep_kernel, ndomain),
         out_shape=part,

time: 13.8 us -> 12.9 us (0.935)
  the two profiles are of different devices: /device:TPU:1 before, /device:TPU:0 now
where the time goes in v2:
time: 12.9 us; the launch traced here: 12.8 us
  starting transfers between devices  5.34 us (41%)
  Pallas kernels  4.67 us (36%)
  waiting for transfers between devices  2.14 us (17%)
  other arithmetic  0.61 us (5%)
    ppermute x3, starting transfers between devices, passed_along(): return lax.ppermute(value, axis, pairs)  5.34 us
    pallas_call x1, Pallas kernels, per_device(): pl.pallas_call(functools.partial(send_kernel, ndomain, sure, plan), out_s...  2.7 us
    ppermute x3, waiting for transfers between devices, passed_along(): return lax.ppermute(value, axis, pairs)  2.14 us
    pallas_call x1, Pallas kernels, per_device(): pl.pallas_call(functools.partial(keep_kernel, ndomain), out_shape=part, i...  1.98 us
    add x1, other arithmetic, per_device(): return functools.reduce(jnp.add, arrived, kept)  0.61 us
  transfers between devices with their start and end apart: 3, of which 2 were waited for; matrix products, arithmetic and copies ran while one was open for 0% of the time, Pallas kernels for 15%

profile of v2, /device:TPU:0, one launch (start us, length us, event | category | flops | bytes accessed | tf_op | source)
XLA Modules:
  0.0 12.8 jit_solution(4773723569594027507)
XLA Ops:
  0.0 2.7 %to_send.1 = (f32[2,4,384]{2,1,0:T(4,128)S(1)}, f32[2,4,384]{2,1,0:T(4,128)S(1)}, f32[2,4,384]{2,1,0:T(4,128)S(1)}, f32[4,2,384]{2,1,0:T(2,128)S(1)}, f32[4,2,38...) custom-call(s32[4,2,16]{2,1,0:T(2,128)} %bitcast.13, s32[16]{0:T(128)} %counts_hbm.3, ...), custom_call_target="tpu_custom_call" | custom-call | tf_op jit(solution)/shard_map/to_send/pallas_call | solution.py:258
  2.7 3.7 %collective-permute-start = (f32[2,4,384]{2,1,0:T(4,128)S(1)}, f32[2,4,384]{2,1,0:T(4,128)S(1)}, u32[]{:S(2)}, u32[]{:S(2)}) collective-permute-start(f32[2,4,384]{2,1,0:T(4,128)S(1)} %get-tuple-element.16), channel_id=1, source_target_pairs={{0,2},{1,3},{2,4},{3,5},{4,6},{5,7},{6,8},{7,9},{8,10},{9,11},{10,... | collective-permute-start | bytes 36872 | tf_op jit(solution)/shard_map/ppermute | solution.py:17
  6.4 0.0 collective-permute-start.1
  6.4 1.6 %collective-permute-start.2 = (f32[2,4,384]{2,1,0:T(4,128)S(1)}, f32[2,4,384]{2,1,0:T(4,128)S(1)}, u32[]{:S(2)}, u32[]{:S(2)}) collective-permute-start(f32[2,4,384]{2,1,0:T(4,128)S(1)} %get-tuple-element.18), channel_id=1, source_target_pairs={{0,1},{1,4},{2,3},{3,6},{4,5},{5,8},{6,7},{7,10},{8,9},{9,12},{10,... | collective-permute-start | bytes 36872 | tf_op jit(solution)/shard_map/ppermute | solution.py:17
  8.1 2.0 %to_keep.1 = f32[2,4,384]{2,1,0:T(4,128)S(1)} custom-call(s32[4,2,16]{2,1,0:T(2,128)} %bitcast.14, s32[16]{0:T(128)} %counts_hbm.3, f32[32]{0:T(128)} %occ_hbm.3, f32[4]{0:T(128)} %shift_hbm.3, f32[4,2,384]{2,1,0:T(2,128)S(1)} %get-tuple-element.12.first_w, f32[4,2,384]{2,1,0:T(2,128)S(1)} %get-tuple-element.13.second_w, ...), custom_call_target="tpu_custom_call" | custom-call | flops 1000000000 | bytes 1000000 | tf_op jit(solution)/shard_map/to_keep/pallas_call | solution.py:287
  10.0 0.4 %collective-permute-done = f32[2,4,384]{2,1,0:T(4,128)S(1)} collective-permute-done((f32[2,4,384]{2,1,0:T(4,128)S(1)}, f32[2,4,384]{2,1,0:T(4,128)S(1)}, u32[]{:S(2)}, u32[]{:S(2)}) %collective-permute-start) | collective-permute-done | bytes 12320 | tf_op jit(solution)/shard_map/ppermute | solution.py:17
  10.4 1.8 %collective-permute-done.1 = f32[2,4,384]{2,1,0:T(4,128)S(1)} collective-permute-done((f32[2,4,384]{2,1,0:T(4,128)S(1)}, f32[2,4,384]{2,1,0:T(4,128)S(1)}, u32[]{:S(2)}, u32[]{:S(2)}) %collective-permute-start.1) | collective-permute-done | bytes 12320 | tf_op jit(solution)/shard_map/ppermute | solution.py:17
  12.2 0.0 collective-permute-done.2
  12.2 0.6 %add_add_fusion = f32[1,8,384]{2,1,0:T(8,128)} fusion(f32[1,8,384]{2,1,0:T(8,128)S(1)} %bitcast.12, f32[1,8,384]{2,1,0:T(8,128)S(1)} %bitcast.11, f32[1,8,384]{2,1,0:T(8,128)S(1)} %bitcast.8, f32[1,8,384]{2,1,0:T(8,128)S(1)} %bitcast.10), kind=kLoop, calls=%fused_computation | loop fusion | flops 9216 | bytes 61440 | tf_op jit(solution)/shard_map/add | solution.py:304
Async XLA Ops:
  2.7 7.7 %collective-permute-start = (f32[2,4,384]{2,1,0:T(4,128)S(1)}, f32[2,4,384]{2,1,0:T(4,128)S(1)}, u32[]{:S(2)}, u32[]{:S(2)}) collective-permute-start(f32[2,4,384]{2,1,0:T(4,128)S(1)} %get-tuple-element.16), channel_id=1, source_target_pairs={{0,2},{1,3},{2,4},{3,5},{4,6},{5,7},{6,8},{7,9},{8,10},{9,11},{10,... | collective-permute-start | bytes 36872 | tf_op jit(solution)/shard_map/ppermute | solution.py:17
  6.4 5.8 %collective-permute-start.1 = (f32[2,4,384]{2,1,0:T(4,128)S(1)}, f32[2,4,384]{2,1,0:T(4,128)S(1)}, u32[]{:S(2)}, u32[]{:S(2)}) collective-permute-start(f32[2,4,384]{2,1,0:T(4,128)S(1)} %get-tuple-element.17), channel_id=1, source_target_pairs={{0,3},{1,2},{2,5},{3,4},{4,7},{5,6},{6,9},{7,8},{8,11},{9,10},{10,... | collective-permute-start | bytes 36872 | tf_op jit(solution)/shard_map/ppermute | solution.py:17
  6.4 5.8 %collective-permute-start.2 = (f32[2,4,384]{2,1,0:T(4,128)S(1)}, f32[2,4,384]{2,1,0:T(4,128)S(1)}, u32[]{:S(2)}, u32[]{:S(2)}) collective-permute-start(f32[2,4,384]{2,1,0:T(4,128)S(1)} %get-tuple-element.18), channel_id=1, source_target_pairs={{0,1},{1,4},{2,3},{3,6},{4,5},{5,8},{6,7},{7,10},{8,9},{9,12},{10,... | collective-permute-start | bytes 36872 | tf_op jit(solution)/shard_map/ppermute | solution.py:17
